TPU v7x, 32 devices: a whole 2x2x4 slice. The times are simulated.
32 devices in a mesh: row: 4 (over z), col: 4 (over x, core), layer: 2 (over y).
Axes of the slice: x: 2, y: 2, z: 4, core: 2. Of those that a mesh axis runs over, the one named last changes fastest.
Arguments:
- density: float32 [2, 2048, 1024], P('layer', 'row', 'col'), may hold values from -6 to 6
- dens_mask: int32 [2, 32, 16], P('layer', 'row', 'col'), may hold values from 0 to 1, as said below
- hamiltonian: float32 [2, 1024, 8192], P('layer', 'row', 'col'), may hold values from -0.375 to 0.375
- ham_mask: int32 [2, 16, 128], P('layer', None, 'col'), may hold values from 0 to 1, as said below
- filter_mask: int32 [32, 128], P('row', 'col'), may hold values from 0 to 1, as said below
Outputs:
- product: float32 [2048, 8192], P('row', ('col', 'layer'))
Inputs may be any that keep to these rules, and one draw needn't show every extreme that they name: `dens_mask`: 1 where a density block is nonzero, else 0. `ham_mask`: 1 where a Hamiltonian block is nonzero, else 0. `filter_mask`: 1 where a result block is kept, else 0.
All inputs are finite; a program needn't handle non-finite values.
Results may differ from a plain program's by a relative error of at most 0.0001.
Values sent between devices are 32-bit elements; how exact they have to be, the bound alone decides.
A program may use at most 128 MiB of HBM per device.

v0:
```python
import jax
import jax.numpy as jnp
from jax import lax
from jax.sharding import PartitionSpec as P

BLOCK = 64


def expand(block_mask):
    widened = jnp.repeat(block_mask.astype(jnp.float32), BLOCK, axis=-2)
    return jnp.repeat(widened, BLOCK, axis=-1)


def shards(density, dens_mask, hamiltonian, ham_mask, filter_mask):
    dens_vals = density * expand(dens_mask)
    ham_count = hamiltonian.shape[1]
    row_ids = lax.axis_index("row") * ham_count + jnp.arange(ham_count, dtype=jnp.int32)
    block_ids = row_ids // BLOCK
    one_hot = (
        block_ids[:, None] == jnp.arange(ham_mask.shape[1], dtype=jnp.int32)[None, :]
    ).astype(jnp.float32)
    picked = jnp.dot(
        one_hot,
        ham_mask[0].astype(jnp.float32),
        precision=lax.Precision.HIGHEST,
        preferred_element_type=jnp.float32,
    )
    ham_vals = hamiltonian * jnp.repeat(picked, BLOCK, axis=1)[None]
    kept = expand(filter_mask)
    ham_group = lax.all_gather(ham_vals, "row", axis=1, tiled=True)
    ham_part = ham_group[0]
    partial_value = jnp.dot(
        lax.all_gather(dens_vals, "col", axis=2, tiled=True)[0],
        ham_part,
        precision=lax.Precision.HIGHEST,
        preferred_element_type=jnp.float32,
    )
    return lax.psum_scatter(partial_value * kept, "layer", scatter_dimension=1, tiled=True)


def solution(mesh):
    return jax.shard_map(
        shards,
        mesh=mesh,
        in_specs=(
            P("layer", "row", "col"),
            P("layer", "row", "col"),
            P("layer", "row", "col"),
            P("layer", None, "col"),
            P("row", "col"),
        ),
        out_specs=P("row", ("col", "layer")),
        check_vma=False,
    )
```

profile of v0, /device:TPU:0, one launch (start us, length us, event | category | flops | bytes accessed | tf_op | source)
XLA Modules:
  0.0 275.9 jit_solution(15941769688353349270)
XLA Ops:
  6.5 0.0 all-gather.3.cloned.1.call-start
  6.5 1.2 copy.8
  7.8 0.7 convert_bitcast_fusion
  8.5 0.1 broadcast_in_dim.21
  8.5 0.1 broadcast_in_dim.22
  8.6 0.9 bitcast_multiply_fusion.1
  9.5 0.0 all-gather.3.cloned.1.call-update
  9.5 0.0 all-gather.5.cloned.1.call-start
  9.6 0.0 copy-start.1
  9.6 1.9 copy.9
  11.5 0.0 copy-done.1
  11.6 0.3 fusion.6
  11.8 1.5 bitcast_multiply_fusion
  13.3 0.0 copy-start
  13.3 0.0 all-gather.5.cloned.1.call-update
  13.3 0.0 reduce-scatter.2.cloned.1.call-start
  13.4 0.6 copy-done
  14.0 0.1 copy.10
  14.1 0.1 broadcast_in_dim.26
  14.2 0.1 reshape.35
  14.3 2.5 broadcast_in_dim.27
  16.8 5.5 %copy.11 = f32[512,2048]{1,0:T(8,128)} copy(f32[512,2048]{0,1:T(8,128)} %bitcast.22) | data formatting | bytes 8388608 | tf_op jit(solution)/shard_map/reshape | solution.py:11
  22.3 12.7 %all-gather.3.cloned.1.call-done = f32[1,512,1024]{1,2,0:T(8,128)} async-done(((f32[1,512,256]{1,2,0:T(8,128)}), f32[1,512,1024]{1,2,0:T(8,128)}) %all-gather.3.cloned.1.call-update) | async-done | bytes 2097168 | tf_op jit(solution)/shard_map/all_gather | solution.py:33
  35.0 151.2 %all-gather.5.cloned.1.call-done = f32[1,1024,2048]{1,2,0:T(8,128)} async-done(((f32[1,256,2048]{1,2,0:T(8,128)}), f32[1,1024,2048]{1,2,0:T(8,128)}) %all-gather.5.cloned.1.call-update) | async-done | bytes 8388624 | tf_op jit(solution)/shard_map/all_gather | solution.py:30
  186.2 30.5 %fusion.2 = f32[512,2048]{1,0:T(8,128)} fusion(f32[512,2048]{1,0:T(8,128)} %copy.11, f32[1,1024,2048]{1,2,0:T(8,128)} %all-gather.5.cloned.1.call-done, f32[1,512,1024]{1,2,0:T(8,128)} %all-gather.3.cloned.1.call-done), kind=kOutput, calls=%fused_computation.2 | convolution fusion | flops 12885950464 | bytes 18874368 | tf_op jit(solution)/shard_map/dot_general | solution.py:32
  216.7 0.0 reduce-scatter.2.cloned.1.call-update
  216.7 52.6 %reduce-scatter.2.cloned.1.call-done = f32[512,1024]{1,0:T(8,128)} async-done(((f32[512,2048]{1,0:T(8,128)}), f32[512,1024]{1,0:T(8,128)}) %reduce-scatter.2.cloned.1.call-update) | async-done | bytes 2097168 | tf_op jit(solution)/shard_map/reduce_scatter | solution.py:38
  (2 shorter events, 0.0 us)
Async XLA Ops:
  6.5 28.4 %all-gather.3.cloned.1.call-start = ((), (), s32[]{:S(2)}) async-start(), calls=%async_computation.1 | async-start | bytes 2621440 | tf_op jit(solution)/shard_map/all_gather | solution.py:33
  9.5 176.7 %all-gather.5.cloned.1.call-start = ((), (), s32[]{:S(2)}) async-start(), calls=%async_computation.2 | async-start | bytes 10485760 | tf_op jit(solution)/shard_map/all_gather | solution.py:30
  9.6 2.0 copy-start.1
  13.3 0.7 copy-start
  13.3 256.0 %reduce-scatter.2.cloned.1.call-start = ((), (), s32[]{:S(2)}) async-start(), calls=%async_computation.3 | async-start | bytes 6291456 | tf_op jit(solution)/shard_map/reduce_scatter | solution.py:38
Sparse Core Ops, SparseCore 0:
  9.6 25.2 all-gather.2
  36.5 149.6 all-gather.4
  216.9 52.4 reduce-scatter.1
where the time goes:
time: 276 us
  waiting for transfers between devices  217 us (79%)
  matrix products  30.8 us (11%)
  between operations  13.2 us (5%)
  local copies, waits for them, and re-layouts  12.2 us (4%)
  other arithmetic  3.05 us (1%)
    all_gather x1, waiting for transfers between devices, shards(): ham_group = lax.all_gather(ham_vals, 'row', axis=1, tiled=True)  151 us
    reduce_scatter x1, waiting for transfers between devices, shards(): lax.psum_scatter(partial_value * kept, 'layer', scatter_dimension=1, tile...  52.6 us
    dot_general x1, matrix products, shards(): jnp.dot(lax.all_gather(dens_vals, 'col', axis=2, tiled=True)[0], ham_part...  30.5 us
    all_gather x1, waiting for transfers between devices, shards(): lax.all_gather(dens_vals, 'col', axis=2, tiled=True)[0]  12.7 us
  transfers between devices with their start and end apart: 3, of which 3 were waited for; matrix products, arithmetic and copies ran while one was open for 4% of the time, Pallas kernels for 0%

commit v1 on v0

v1 whole, which is shorter than its diff:
```python
import functools

import jax
import jax.numpy as jnp
from jax import lax
from jax.experimental import pallas as pl
from jax.experimental.pallas import tpu as pltpu
from jax.sharding import PartitionSpec as P

BLOCK = 64
CHUNKS = 4


def expand(block_mask):
    widened = jnp.repeat(block_mask.astype(jnp.float32), BLOCK, axis=-2)
    return jnp.repeat(widened, BLOCK, axis=-1)


def masked_ham(hamiltonian, ham_mask):
    blocks = hamiltonian.shape[1] // BLOCK
    mine = lax.dynamic_slice_in_dim(ham_mask[0], lax.axis_index("row") * blocks, blocks, 0)
    wide = jnp.repeat(mine.astype(jnp.float32), BLOCK, axis=1)
    ham = hamiltonian[0].reshape(blocks, BLOCK, -1) * wide[:, None, :]
    return ham.reshape(hamiltonian.shape[1:])


def split(x):
    high = x.astype(jnp.bfloat16)
    return high, (x - high.astype(jnp.float32)).astype(jnp.bfloat16)


def kernel(
    d_ref, h_ref, out_ref,
    dbuf, hbuf, dhi, dlo, hhi, hlo, mine, ends,
    d_sem, h_sem, res_sem, send_sem, res_send, local_sem, y_sem,
):
    r, c, l = lax.axis_index("row"), lax.axis_index("col"), lax.axis_index("layer")
    rows, width = d_ref.shape
    depth = h_ref.shape[0]
    cols = out_ref.shape[1]
    cw = cols // CHUNKS
    across = (c + 2) % 4
    sibling = c + 1 - 2 * (c % 2)
    other = 1 - l
    is_hub = jnp.logical_and(r > 0, r < 3)

    def at(row, col, layer):
        return {"row": row, "col": col, "layer": layer}

    def send(src, dst, sem, recv, where):
        copy = pltpu.make_async_remote_copy(
            src_ref=src, dst_ref=dst, send_sem=sem, recv_sem=recv,
            device_id=where, device_id_type=pl.DeviceIdType.MESH,
        )
        copy.start()
        return copy

    def arrived(ref, recv):
        pltpu.make_async_remote_copy(
            src_ref=ref, dst_ref=ref, send_sem=send_sem.at[0], recv_sem=recv,
            device_id=at(r, c, other), device_id_type=pl.DeviceIdType.MESH,
        ).wait_recv()

    def ham_rows(row, layer):
        return pl.ds(pl.multiple_of((row * 2 + layer) * depth, depth), depth)

    def chunk(j):
        return pl.ds(pl.multiple_of(j * cw, cw), cw)

    def piece(slot, half):
        return dbuf.at[slot, pl.ds(half * rows, rows), :]

    def ham_from(layer, j):
        return h_ref.at[:, pl.ds(pl.multiple_of(layer * cols + j * cw, cw), cw)]

    barrier = pltpu.get_barrier_semaphore()

    def greet(partners):
        for where in partners:
            pl.semaphore_signal(barrier, inc=1, device_id=where, device_id_type=pl.DeviceIdType.MESH)
        pl.semaphore_wait(barrier, len(partners))

    @pl.when(jnp.logical_not(is_hub))
    def _():
        hub = 1 + r // 3
        greet([at(hub, c, l), at(hub, c, other)])
        first = send(d_ref, piece(c * 2 + l, 1), send_sem.at[0], d_sem.at[c * 2 + l, 1], at(hub, c, l))
        first.wait_send()
        sent = []
        for j in range(CHUNKS):
            for layer, k in ((l, 0), (other, 1)):
                sent.append(send(
                    ham_from(layer, j), hbuf.at[ham_rows(r, l), chunk(j)],
                    send_sem.at[1 + 2 * j + k], h_sem.at[r, l, j], at(hub, c, layer),
                ))
        kept = []
        for j in range(CHUNKS):
            arrived(ends.at[:, chunk(j)], res_sem.at[j])
            keep = pltpu.make_async_copy(ends.at[:, chunk(j)], out_ref.at[:, chunk(j)], local_sem.at[j])
            keep.start()
            kept.append(keep)
        for copy in sent:
            copy.wait_send()
        for copy in kept:
            copy.wait()

    @pl.when(is_hub)
    def _():
        far, end = 3 - r, 3 * r - 3
        far_end = 3 - end
        greet([
            at(r, c, other), at(r, across, l), at(r, sibling, l),
            at(end, c, l), at(end, c, other), at(far, c, l), at(far, c, other),
        ])
        own = c * 2 + l
        sent = []

        def push(src, dst, recv, where):
            sent.append(send(src, dst, send_sem.at[len(sent)], recv, where))

        def absorb(slot, half):
            def tile(i, _):
                at_rows = pl.ds(pl.multiple_of(half * rows + i * 128, 128), 128)
                high, low = split(dbuf[slot, at_rows, :])
                at_cols = pl.ds(pl.multiple_of(slot * width, width), width)
                dhi[at_rows, at_cols] = high
                dlo[at_rows, at_cols] = low
                return 0

            lax.fori_loop(0, rows // 128, tile, 0)

        def pass_on(src, slot, half, partners):
            for where in partners:
                push(src, piece(slot, half), d_sem.at[slot, half], where)

        y, x, s = at(r, c, other), at(r, across, l), at(r, sibling, l)

        local_d = pltpu.make_async_copy(d_ref, piece(own, 0), local_sem.at[0])
        local_d.start()
        local_h = pltpu.make_async_copy(
            h_ref.at[:, pl.ds(pl.multiple_of(l * cols, cols), cols)],
            hbuf.at[ham_rows(r, l), :], local_sem.at[1],
        )
        local_h.start()
        pass_on(d_ref, own, 0, (y, x, s))
        for j in range(CHUNKS):
            for layer in (l, other):
                push(
                    ham_from(layer, j), hbuf.at[ham_rows(r, l), chunk(j)],
                    h_sem.at[r, l, j], at(far, c, layer),
                )
        local_d.wait()
        absorb(own, 0)

        def take(slot, half, partners):
            arrived(piece(slot, half), d_sem.at[slot, half])
            pass_on(piece(slot, half), slot, half, partners)
            absorb(slot, half)

        take(own, 1, (y, x, s))
        push(
            h_ref.at[:, pl.ds(pl.multiple_of(other * cols, cols), cols)],
            hbuf.at[ham_rows(r, l), :], y_sem, y,
        )
        take(c * 2 + other, 0, (x, s))

        def relay(j):
            for layer in range(2):
                ref = hbuf.at[ham_rows(end, layer), chunk(j)]
                arrived(ref, h_sem.at[end, layer, j])
                push(ref, ref, h_sem.at[end, layer, j], at(far, c, l))

        relay(0)
        take(c * 2 + other, 1, (x, s))
        take(across * 2 + l, 0, (s,))
        for j in range(1, CHUNKS // 2):
            relay(j)
        take(across * 2 + l, 1, (s,))
        take(across * 2 + other, 0, (s,))
        for j in range(CHUNKS // 2, CHUNKS):
            relay(j)
        take(across * 2 + other, 1, (s,))
        far_sibling = (sibling + 2) % 4
        for col in (sibling, far_sibling):
            for layer in (l, other):
                for half in range(2):
                    take(col * 2 + layer, half, ())
        local_h.wait()
        arrived(hbuf.at[ham_rows(r, other), :], y_sem)

        def rows_of(first, target, j):
            def tile(i, _):
                at_rows = pl.ds(pl.multiple_of(first + i * 256, 256), 256)
                high = dhi[at_rows, :]
                total = jnp.dot(high, hhi[...], preferred_element_type=jnp.float32)
                total += jnp.dot(high, hlo[...], preferred_element_type=jnp.float32)
                total += jnp.dot(dlo[at_rows, :], hhi[...], preferred_element_type=jnp.float32)
                target[pl.ds(pl.multiple_of(i * 256, 256), 256), chunk(j)] = total
                return 0

            lax.fori_loop(0, rows // 256, tile, 0)

        def result(j):
            return pltpu.make_async_remote_copy(
                src_ref=ends.at[:, chunk(j)], dst_ref=ends.at[:, chunk(j)],
                send_sem=res_send.at[j], recv_sem=res_sem.at[j],
                device_id=at(end, c, l), device_id_type=pl.DeviceIdType.MESH,
            )

        def keep(j):
            return pltpu.make_async_copy(mine.at[:, chunk(j)], out_ref.at[:, chunk(j)], local_sem.at[2 + j])

        def step(j, _):
            for row in (far, far_end):
                for layer in range(2):
                    arrived(hbuf.at[ham_rows(row, layer), chunk(j)], h_sem.at[row, layer, j])

            def part(i, _):
                at_rows = pl.ds(pl.multiple_of(i * 256, 256), 256)
                high, low = split(hbuf[at_rows, chunk(j)])
                hhi[at_rows, :] = high
                hlo[at_rows, :] = low
                return 0

            lax.fori_loop(0, hbuf.shape[0] // 256, part, 0)
            rows_of(rows, ends, j)
            result(j).start()
            rows_of(0, mine, j)
            keep(j).start()
            return 0

        lax.fori_loop(0, CHUNKS, step, 0)
        for copy in sent:
            copy.wait_send()
        for j in range(CHUNKS):
            result(j).wait_send()
            keep(j).wait()


def product_of(dens, ham, layers, grid_cols):
    rows, width = dens.shape
    depth, ham_cols = ham.shape
    cols = ham_cols // layers
    inner = layers * grid_cols * width
    f32, bf16 = jnp.float32, jnp.bfloat16
    dma = pltpu.SemaphoreType.DMA
    return pl.pallas_call(
        kernel,
        out_shape=jax.ShapeDtypeStruct((rows, cols), f32),
        in_specs=[pl.BlockSpec(memory_space=pl.ANY)] * 2,
        out_specs=pl.BlockSpec(memory_space=pl.ANY),
        scratch_shapes=[
            pltpu.VMEM((layers * grid_cols, 2 * rows, width), f32),
            pltpu.VMEM((inner, cols), f32),
            pltpu.VMEM((2 * rows, inner), bf16),
            pltpu.VMEM((2 * rows, inner), bf16),
            pltpu.VMEM((inner, cols // CHUNKS), bf16),
            pltpu.VMEM((inner, cols // CHUNKS), bf16),
            pltpu.VMEM((rows, cols), f32),
            pltpu.VMEM((rows, cols), f32),
            dma((layers * grid_cols, 2)),
            dma((4, 2, CHUNKS)),
            dma((CHUNKS,)),
            dma((16 + 4 * CHUNKS,)),
            dma((CHUNKS,)),
            dma((2 + CHUNKS,)),
            dma,
        ],
        compiler_params=pltpu.CompilerParams(
            collective_id=0, has_side_effects=True, vmem_limit_bytes=48 * 2**20
        ),
    )(dens, ham)


def lined_up(density, dens_mask, hamiltonian, ham_mask, filter_mask, *, layers, grid_cols):
    dens = density[0] * expand(dens_mask[0])
    ham = masked_ham(hamiltonian, ham_mask)
    total = product_of(dens, ham, layers, grid_cols)
    kept_blocks = filter_mask.shape[1] // layers
    kept = lax.dynamic_slice_in_dim(filter_mask, lax.axis_index("layer") * kept_blocks, kept_blocks, 1)
    wide = jnp.repeat(kept.astype(jnp.float32), BLOCK, axis=1)
    out = total.reshape(-1, BLOCK, total.shape[1]) * wide[:, None, :]
    return out.reshape(total.shape)


def gathered(density, dens_mask, hamiltonian, ham_mask, filter_mask):
    dens = lax.all_gather(density * expand(dens_mask), "col", axis=2, tiled=True)[0]
    ham = lax.all_gather(masked_ham(hamiltonian, ham_mask), "row", axis=0, tiled=True)
    part = jnp.dot(dens, ham, precision=lax.Precision.HIGHEST, preferred_element_type=jnp.float32)
    return lax.psum_scatter(part * expand(filter_mask), "layer", scatter_dimension=1, tiled=True)


def solution(mesh):
    sizes = dict(mesh.shape)
    layers, grid_cols = sizes["layer"], sizes["col"]
    body = gathered
    if sizes == {"row": 4, "col": 4, "layer": 2}:
        body = functools.partial(lined_up, layers=layers, grid_cols=grid_cols)
    return jax.shard_map(
        body,
        mesh=mesh,
        in_specs=(
            P("layer", "row", "col"),
            P("layer", "row", "col"),
            P("layer", "row", "col"),
            P("layer", None, "col"),
            P("row", "col"),
        ),
        out_specs=P("row", ("col", "layer")),
        check_vma=False,
    )
```

time: 276 us -> 153 us (0.55)
  waiting for transfers between devices: 217 us -> 0 us
  Pallas kernels: 0 us -> 145 us
  matrix products: 30.8 us -> 0 us
  between operations: 13.2 us -> 0.08 us
  local copies, waits for them, and re-layouts: 12.2 us -> 2.35 us
    all_gather x2 -> x0, waiting for transfers between devices: 164 us -> none  [the longest x1 151 us: shards(): ham_group = lax.all_gather(ham_vals, 'row', axis=1, tiled=True)]
    pallas_call x0 -> x1, Pallas kernels: none -> 145 us  [product_of(): pl.pallas_call(kernel, out_shape=jax.ShapeDtypeStruct((rows, cols), f32),...]
    reduce_scatter x1 -> x0, waiting for transfers between devices: 52.6 us -> none  [shards(): lax.psum_scatter(partial_value * kept, 'layer', scatter_dimension=1, tile...]
    dot_general x2 -> x0, matrix products: 30.8 us -> none  [the longest x1 30.5 us: shards(): jnp.dot(lax.all_gather(dens_vals, 'col', axis=2, tiled=True)[0], ham_part...]
    reshape x1, local copies, waits for them, and re-layouts: 5.5 us -> 0.2 us  [expand(): return jnp.repeat(widened, BLOCK, axis=-1)]
  transfers between devices with their start and end apart: 3 -> 0, of which waited for: 3 -> 0; matrix products, arithmetic and copies ran while one was open for 4% -> 0% of each run, Pallas kernels for 0% -> 0%
where the time goes in v1:
time: 153 us
  Pallas kernels  145 us (95%)
  other arithmetic  5.61 us (4%)
  local copies, waits for them, and re-layouts  2.35 us (2%)
    pallas_call x1, Pallas kernels, product_of(): pl.pallas_call(kernel, out_shape=jax.ShapeDtypeStruct((rows, cols), f32),...  145 us
    mul x1, other arithmetic, masked_ham(): ham = hamiltonian[0].reshape(blocks, BLOCK, -1) * wide[:, None, :]  3.26 us

profile of v1, /device:TPU:0, one launch (start us, length us, event | category | flops | bytes accessed | tf_op | source)
XLA Modules:
  0.0 152.6 jit_solution(13176359847953733486)
XLA Ops:
  0.0 0.7 convert_bitcast_fusion
  0.7 0.1 broadcast_in_dim.14
  0.8 0.1 mul.37
  0.9 0.0 copy-start.3
  0.9 0.0 copy-start.1
  0.9 3.3 %bitcast_multiply_fusion.1.h_ref = f32[256,2048]{1,0:T(8,128)} fusion(f32[1,256,2048]{2,1,0:T(8,128)} %param.7, f32[4,2048]{1,0:T(4,128)S(1)} %mul.37), kind=kLoop, calls=%fused_computation.1 | loop fusion | flops 524288 | bytes 4227072 | tf_op jit(solution)/shard_map/mul | solution.py:23
  4.2 0.0 copy-done.3
  4.2 0.1 broadcast_in_dim.12
  4.2 0.1 reshape.17
  4.3 0.1 broadcast_in_dim.13
  4.4 0.2 copy.7
  4.6 0.0 copy-done.1
  4.6 0.1 bitcast_multiply_fusion.2.d_ref
  4.7 0.0 copy-start
  4.7 1.6 %copy-done = f32[256,2048]{1,0:T(8,128)S(1)} copy-done((f32[256,2048]{1,0:T(8,128)S(1)}, f32[256,2048]{1,0:T(8,128)}, u32[]{:S(2)}) %copy-start) | copy-done | bytes 2097176
  6.3 0.0 copy-start.2
  6.3 144.6 %shard_map.55 = f32[512,1024]{1,0:T(8,128)S(1)} custom-call(f32[512,256]{1,0:T(8,128)S(1)} %bitcast_multiply_fusion.2.d_ref, f32[256,2048]{1,0:T(8,128)S(1)} %copy-done), custom_call_target="tpu_custom_call" | custom-call | tf_op jit(solution)/shard_map/pallas_call | solution.py:247
  150.8 0.0 copy-done.2
  150.9 0.1 dynamic-slice_convert_fusion
  150.9 0.1 broadcast_in_dim.15
  151.0 0.1 mul.42
  151.1 1.5 bitcast_multiply_fusion
  (1 shorter events, 0.0 us)
Async XLA Ops:
  0.9 3.3 %copy-start.3 = (s32[1,8,4]{1,2,0:T(4,128)S(1)}, s32[1,8,4]{1,2,0:T(4,128)}, u32[]{:S(2)}) copy-start(s32[1,8,4]{1,2,0:T(4,128)} %param.6) | copy-start | bytes 388
  0.9 3.7 %copy-start.1 = (f32[1,512,256]{2,1,0:T(8,128)S(1)}, f32[1,512,256]{2,1,0:T(8,128)}, u32[]{:S(2)}) copy-start(f32[1,512,256]{2,1,0:T(8,128)} %param.5) | copy-start | bytes 1572868
  4.7 1.6 %copy-start = (f32[256,2048]{1,0:T(8,128)S(1)}, f32[256,2048]{1,0:T(8,128)}, u32[]{:S(2)}) copy-start(f32[256,2048]{1,0:T(8,128)} %bitcast_multiply_fusion.1.h_ref) | copy-start | bytes 6291460
  6.3 144.6 %copy-start.2 = (s32[8,32]{1,0:T(8,128)S(1)}, s32[8,32]{1,0:T(8,128)}, u32[]{:S(2)}) copy-start(s32[8,32]{1,0:T(8,128)} %param.9) | copy-start | bytes 3076

commit v2 on v1

v2 whole, which is shorter than its diff:
```python
import functools

import jax
import jax.numpy as jnp
from jax import lax
from jax.experimental import pallas as pl
from jax.experimental.pallas import tpu as pltpu
from jax.sharding import PartitionSpec as P

BLOCK = 64


def expand(block_mask):
    widened = jnp.repeat(block_mask.astype(jnp.float32), BLOCK, axis=-2)
    return jnp.repeat(widened, BLOCK, axis=-1)


def masked_ham(hamiltonian, ham_mask):
    blocks = hamiltonian.shape[1] // BLOCK
    mine = lax.dynamic_slice_in_dim(ham_mask[0], lax.axis_index("row") * blocks, blocks, 0)
    wide = jnp.repeat(mine.astype(jnp.float32), BLOCK, axis=1)
    ham = hamiltonian[0].reshape(blocks, BLOCK, -1) * wide[:, None, :]
    return ham.reshape(hamiltonian.shape[1:])


def split(x):
    high = x.astype(jnp.bfloat16)
    return high, (x - high.astype(jnp.float32)).astype(jnp.bfloat16)


def kernel(
    d_ref, h_ref, out_ref,
    dbuf, hbuf, dhi, dlo, hhi, hlo, mine, ends,
    d_sem, h_sem, res_sem, send_sem, res_send, local_sem,
):
    r, c, l = lax.axis_index("row"), lax.axis_index("col"), lax.axis_index("layer")
    rows, width = d_ref.shape
    depth = h_ref.shape[0]
    cols = out_ref.shape[1]
    spans = chunk_spans(cols)
    across = (c + 2) % 4
    sibling = c + 1 - 2 * (c % 2)
    other = 1 - l
    own, yours = c * 2 + l, c * 2 + other
    is_hub = jnp.logical_and(r > 0, r < 3)

    def at(row, col, layer):
        return {"row": row, "col": col, "layer": layer}

    def arrived(ref, recv):
        pltpu.make_async_remote_copy(
            src_ref=ref, dst_ref=ref, send_sem=send_sem.at[0], recv_sem=recv,
            device_id=at(r, c, other), device_id_type=pl.DeviceIdType.MESH,
        ).wait_recv()

    def ham_rows(row, layer):
        return pl.ds(pl.multiple_of((row * 2 + layer) * depth, depth), depth)

    def chunk(j):
        return pl.ds(*spans[j])

    def piece(slot, half):
        return dbuf.at[slot, pl.ds(half * rows, rows), :]

    def ham_from(layer, j):
        first, wide = spans[j]
        return h_ref.at[:, pl.ds(pl.multiple_of(layer * cols + first, 128), wide)]

    def held(row, layer, j):
        return hbuf.at[ham_rows(row, layer), chunk(j)]

    sent = []

    def push(src, dst, recv, where):
        copy = pltpu.make_async_remote_copy(
            src_ref=src, dst_ref=dst, send_sem=send_sem.at[len(sent)], recv_sem=recv,
            device_id=where, device_id_type=pl.DeviceIdType.MESH,
        )
        copy.start()
        sent.append(copy)

    barrier = pltpu.get_barrier_semaphore()

    def greet(partners):
        for where in partners:
            pl.semaphore_signal(barrier, inc=1, device_id=where, device_id_type=pl.DeviceIdType.MESH)
        pl.semaphore_wait(barrier, len(partners))

    y = at(r, c, other)

    @pl.when(jnp.logical_not(is_hub))
    def _():
        sent.clear()
        hub = at(1 + r // 3, c, l)
        greet([hub, y])
        push(d_ref, piece(own, 1), d_sem.at[own, 1], hub)
        push(d_ref, piece(own, 1), d_sem.at[own, 1], y)
        for j in range(len(spans)):
            push(ham_from(other, j), held(r, l, j), h_sem.at[r, l, j], y)
        arrived(piece(yours, 1), d_sem.at[yours, 1])
        push(piece(yours, 1), piece(yours, 1), d_sem.at[yours, 1], hub)
        sent[0].wait_send()
        last = len(sent) - 1
        for j in range(len(spans)):
            push(ham_from(l, j), held(r, l, j), h_sem.at[r, l, j], hub)
            arrived(held(r, other, j), h_sem.at[r, other, j])
            push(held(r, other, j), held(r, other, j), h_sem.at[r, other, j], hub)
            if j == 0:
                sent[last].wait_send()
            else:
                sent[last + 2 * j - 1].wait_send()
                sent[last + 2 * j].wait_send()
        waited = {0} | set(range(last, len(sent) - 2))
        kept = []
        for j in range(len(spans)):
            arrived(ends.at[:, chunk(j)], res_sem.at[j])
            keep = pltpu.make_async_copy(ends.at[:, chunk(j)], out_ref.at[:, chunk(j)], local_sem.at[j])
            keep.start()
            kept.append(keep)
        for i, copy in enumerate(sent):
            if i not in waited:
                copy.wait_send()
        for copy in kept:
            copy.wait()

    @pl.when(is_hub)
    def _():
        sent.clear()
        end_row, far_row = 3 * r - 3, 3 - r
        far_end = 3 - end_row
        x, s = at(r, across, l), at(r, sibling, l)
        end, far = at(end_row, c, l), at(far_row, c, l)
        greet([y, x, s, end, far])

        def absorb(slot, half):
            def tile(i, _):
                at_rows = pl.ds(pl.multiple_of(half * rows + i * 128, 128), 128)
                high, low = split(dbuf[slot, at_rows, :])
                at_cols = pl.ds(pl.multiple_of(slot * width, width), width)
                dhi[at_rows, at_cols] = high
                dlo[at_rows, at_cols] = low
                return 0

            lax.fori_loop(0, rows // 128, tile, 0)

        def take(slot, half, *partners):
            arrived(piece(slot, half), d_sem.at[slot, half])
            for where in partners:
                push(piece(slot, half), piece(slot, half), d_sem.at[slot, half], where)
            absorb(slot, half)

        def straight(j):
            push(ham_from(l, j), held(r, l, j), h_sem.at[r, l, j], far)

        def relay(row, layer, j):
            arrived(held(row, layer, j), h_sem.at[row, layer, j])
            push(held(row, layer, j), held(row, layer, j), h_sem.at[row, layer, j], far)

        def relay_end(j):
            relay(end_row, l, j)
            relay(end_row, other, j)

        def split_ham(j):
            for row in (far_row, far_end):
                for layer in range(2):
                    arrived(held(row, layer, j), h_sem.at[row, layer, j])

            def part(i, _):
                at_rows = pl.ds(pl.multiple_of(i * 256, 256), 256)
                high, low = split(hbuf[at_rows, chunk(j)])
                hhi[at_rows, chunk(j)] = high
                hlo[at_rows, chunk(j)] = low
                return 0

            lax.fori_loop(0, hbuf.shape[0] // 256, part, 0)

        def rows_of(half, target, j):
            def tile(i, _):
                at_rows = pl.ds(pl.multiple_of(half * rows + i * 256, 256), 256)
                high = dhi[at_rows, :]
                total = jnp.dot(high, hhi[:, chunk(j)], preferred_element_type=jnp.float32)
                total += jnp.dot(high, hlo[:, chunk(j)], preferred_element_type=jnp.float32)
                total += jnp.dot(dlo[at_rows, :], hhi[:, chunk(j)], preferred_element_type=jnp.float32)
                target[pl.ds(pl.multiple_of(i * 256, 256), 256), chunk(j)] = total
                return 0

            lax.fori_loop(0, rows // 256, tile, 0)

        results, kept = [], []

        def end_rows(j):
            split_ham(j)
            rows_of(1, ends, j)
            copy = pltpu.make_async_remote_copy(
                src_ref=ends.at[:, chunk(j)], dst_ref=ends.at[:, chunk(j)],
                send_sem=res_send.at[j], recv_sem=res_sem.at[j],
                device_id=end, device_id_type=pl.DeviceIdType.MESH,
            )
            copy.start()
            results.append(copy)

        def own_rows(j):
            rows_of(0, mine, j)
            copy = pltpu.make_async_copy(mine.at[:, chunk(j)], out_ref.at[:, chunk(j)], local_sem.at[2 + j])
            copy.start()
            kept.append(copy)

        local_d = pltpu.make_async_copy(d_ref, piece(own, 0), local_sem.at[0])
        local_d.start()
        for where in (y, x, s):
            push(d_ref, piece(own, 0), d_sem.at[own, 0], where)
        straight(0)
        straight(1)
        for j in range(len(spans)):
            push(ham_from(other, j), held(r, l, j), h_sem.at[r, l, j], y)
        local_h = pltpu.make_async_copy(
            h_ref.at[:, pl.ds(pl.multiple_of(l * cols, cols), cols)],
            hbuf.at[ham_rows(r, l), :], local_sem.at[1],
        )
        local_h.start()
        local_d.wait()
        absorb(own, 0)
        take(own, 1, x, s)
        relay(r, other, 0)
        relay(r, other, 1)
        straight(2)
        take(yours, 1, x, s)
        relay(r, other, 2)
        straight(3)
        take(yours, 0, x, s)
        relay_end(0)
        take(across * 2 + l, 1, s)
        relay(r, other, 3)
        relay_end(1)
        take(across * 2 + other, 1, s)
        straight(4)
        relay(r, other, 4)
        away = (sibling + 2) % 4
        beside = [col * 2 + layer for col in (sibling, away) for layer in (l, other)]
        for slot in beside:
            take(slot, 1)
        local_h.wait()
        end_rows(0)
        take(across * 2 + l, 0, s)
        take(across * 2 + other, 0, s)
        relay_end(2)
        end_rows(1)
        relay_end(3)
        for slot in beside:
            take(slot, 0)
        own_rows(0)
        relay_end(4)
        own_rows(1)
        for j in range(2, len(spans)):
            end_rows(j)
            own_rows(j)
        for copy in sent + results:
            copy.wait_send()
        for copy in kept:
            copy.wait()


def chunk_spans(cols):
    quarter = cols // 4
    widths = [quarter] * 3 + [quarter // 2] * 2
    return [(sum(widths[:j]), width) for j, width in enumerate(widths)]


def product_of(dens, ham, layers, grid_cols):
    rows, width = dens.shape
    depth, ham_cols = ham.shape
    cols = ham_cols // layers
    inner = layers * grid_cols * width
    chunks = len(chunk_spans(cols))
    f32, bf16 = jnp.float32, jnp.bfloat16
    dma = pltpu.SemaphoreType.DMA
    return pl.pallas_call(
        kernel,
        out_shape=jax.ShapeDtypeStruct((rows, cols), f32),
        in_specs=[pl.BlockSpec(memory_space=pl.ANY)] * 2,
        out_specs=pl.BlockSpec(memory_space=pl.ANY),
        scratch_shapes=[
            pltpu.VMEM((layers * grid_cols, 2 * rows, width), f32),
            pltpu.VMEM((inner, cols), f32),
            pltpu.VMEM((2 * rows, inner), bf16),
            pltpu.VMEM((2 * rows, inner), bf16),
            pltpu.VMEM((inner, cols), bf16),
            pltpu.VMEM((inner, cols), bf16),
            pltpu.VMEM((rows, cols), f32),
            pltpu.VMEM((rows, cols), f32),
            dma((layers * grid_cols, 2)),
            dma((4, 2, chunks)),
            dma((chunks,)),
            dma((16 + 5 * chunks,)),
            dma((chunks,)),
            dma((2 + chunks,)),
        ],
        compiler_params=pltpu.CompilerParams(
            collective_id=0, has_side_effects=True, vmem_limit_bytes=52 * 2**20
        ),
    )(dens, ham)


def lined_up(density, dens_mask, hamiltonian, ham_mask, filter_mask, *, layers, grid_cols):
    dens = density[0] * expand(dens_mask[0])
    ham = masked_ham(hamiltonian, ham_mask)
    total = product_of(dens, ham, layers, grid_cols)
    kept_blocks = filter_mask.shape[1] // layers
    kept = lax.dynamic_slice_in_dim(filter_mask, lax.axis_index("layer") * kept_blocks, kept_blocks, 1)
    wide = jnp.repeat(kept.astype(jnp.float32), BLOCK, axis=1)
    out = total.reshape(-1, BLOCK, total.shape[1]) * wide[:, None, :]
    return out.reshape(total.shape)


def gathered(density, dens_mask, hamiltonian, ham_mask, filter_mask):
    dens = lax.all_gather(density * expand(dens_mask), "col", axis=2, tiled=True)[0]
    ham = lax.all_gather(masked_ham(hamiltonian, ham_mask), "row", axis=0, tiled=True)
    part = jnp.dot(dens, ham, precision=lax.Precision.HIGHEST, preferred_element_type=jnp.float32)
    return lax.psum_scatter(part * expand(filter_mask), "layer", scatter_dimension=1, tiled=True)


def solution(mesh):
    sizes = dict(mesh.shape)
    layers, grid_cols = sizes["layer"], sizes["col"]
    body = gathered
    if sizes == {"row": 4, "col": 4, "layer": 2}:
        body = functools.partial(lined_up, layers=layers, grid_cols=grid_cols)
    return jax.shard_map(
        body,
        mesh=mesh,
        in_specs=(
            P("layer", "row", "col"),
            P("layer", "row", "col"),
            P("layer", "row", "col"),
            P("layer", None, "col"),
            P("row", "col"),
        ),
        out_specs=P("row", ("col", "layer")),
        check_vma=False,
    )
```

time: 153 us -> 125 us (0.82)
  Pallas kernels: 145 us -> 117 us
  other arithmetic: 5.61 us -> 7.33 us
  local copies, waits for them, and re-layouts: 2.35 us -> 0.76 us
    pallas_call x1, Pallas kernels: 145 us -> 117 us  [product_of(): pl.pallas_call(kernel, out_shape=jax.ShapeDtypeStruct((rows, cols), f32),...]
    mul x1, other arithmetic: 1.51 us -> 3.23 us  [lined_up(): out = total.reshape(-1, BLOCK, total.shape[1]) * wide[:, None, :]]
    unnamed x8 -> x6, local copies, waits for them, and re-layouts: 1.6 us -> 0.02 us
where the time goes in v2:
time: 125 us
  Pallas kernels  117 us (94%)
  other arithmetic  7.33 us (6%)
    pallas_call x1, Pallas kernels, product_of(): pl.pallas_call(kernel, out_shape=jax.ShapeDtypeStruct((rows, cols), f32),...  117 us
    mul x1, other arithmetic, masked_ham(): ham = hamiltonian[0].reshape(blocks, BLOCK, -1) * wide[:, None, :]  3.26 us
    mul x1, other arithmetic, lined_up(): out = total.reshape(-1, BLOCK, total.shape[1]) * wide[:, None, :]  3.23 us

profile of v2, /device:TPU:0, one launch (start us, length us, event | category | flops | bytes accessed | tf_op | source)
XLA Modules:
  0.0 125.2 jit_solution(1192453437792950039)
XLA Ops:
  0.0 0.7 convert_bitcast_fusion
  0.7 0.1 broadcast_in_dim.14
  0.8 0.1 mul.37
  0.9 0.0 copy-start.2
  0.9 0.0 copy-start
  0.9 3.3 %bitcast_multiply_fusion.1.h_ref = f32[256,2048]{1,0:T(8,128)} fusion(f32[1,256,2048]{2,1,0:T(8,128)} %param.7, f32[4,2048]{1,0:T(4,128)S(1)} %mul.37), kind=kLoop, calls=%fused_computation.1 | loop fusion | flops 524288 | bytes 4227072 | tf_op jit(solution)/shard_map/mul | solution.py:22
  4.2 0.0 copy-done.2
  4.2 0.1 broadcast_in_dim.12
  4.2 0.1 reshape.17
  4.3 0.1 broadcast_in_dim.13
  4.4 0.2 copy.7
  4.6 0.0 copy-done
  4.6 0.1 bitcast_multiply_fusion.2.d_ref
  4.7 0.0 copy-start.1
  4.7 117.1 %shard_map.55 = f32[512,1024]{1,0:T(8,128)} custom-call(f32[512,256]{1,0:T(8,128)S(1)} %bitcast_multiply_fusion.2.d_ref, f32[256,2048]{1,0:T(8,128)} %bitcast_multiply_fusion.1.h_ref), custom_call_target="tpu_custom_call" | custom-call | tf_op jit(solution)/shard_map/pallas_call | solution.py:277
  121.7 0.0 copy-done.1
  121.8 0.1 dynamic-slice_convert_fusion
  121.8 0.1 broadcast_in_dim.15
  121.9 0.1 mul.42
  122.0 3.2 %bitcast_multiply_fusion = f32[512,1024]{1,0:T(8,128)} fusion(f32[512,1024]{1,0:T(8,128)} %shard_map.55, f32[8,1024]{1,0:T(8,128)S(1)} %mul.42), kind=kLoop, calls=%fused_computation | loop fusion | flops 524288 | bytes 4227072 | tf_op jit(solution)/shard_map/mul | solution.py:311
  (1 shorter events, 0.0 us)
Async XLA Ops:
  0.9 3.3 %copy-start.2 = (s32[1,8,4]{1,2,0:T(4,128)S(1)}, s32[1,8,4]{1,2,0:T(4,128)}, u32[]{:S(2)}) copy-start(s32[1,8,4]{1,2,0:T(4,128)} %param.6) | copy-start | bytes 388
  0.9 3.7 %copy-start = (f32[1,512,256]{2,1,0:T(8,128)S(1)}, f32[1,512,256]{2,1,0:T(8,128)}, u32[]{:S(2)}) copy-start(f32[1,512,256]{2,1,0:T(8,128)} %param.5) | copy-start | bytes 1572868
  4.7 117.1 %copy-start.1 = (s32[8,32]{1,0:T(8,128)S(1)}, s32[8,32]{1,0:T(8,128)}, u32[]{:S(2)}) copy-start(s32[8,32]{1,0:T(8,128)} %param.9) | copy-start | bytes 3076

commit v3 on v2

--- a/solution.py
+++ b/solution.py
@@ -226,34 +226,37 @@
         straight(2)
         take(yours, 1, x, s)
         relay(r, other, 2)
-        straight(3)
         take(yours, 0, x, s)
         relay_end(0)
         take(across * 2 + l, 1, s)
-        relay(r, other, 3)
+        straight(3)
         relay_end(1)
         take(across * 2 + other, 1, s)
-        straight(4)
-        relay(r, other, 4)
+        relay(r, other, 3)
         away = (sibling + 2) % 4
         beside = [col * 2 + layer for col in (sibling, away) for layer in (l, other)]
         for slot in beside:
             take(slot, 1)
         local_h.wait()
         end_rows(0)
+        relay_end(2)
         take(across * 2 + l, 0, s)
         take(across * 2 + other, 0, s)
-        relay_end(2)
         end_rows(1)
         relay_end(3)
+        straight(4)
+        relay(r, other, 4)
         for slot in beside:
             take(slot, 0)
         own_rows(0)
         relay_end(4)
         own_rows(1)
-        for j in range(2, len(spans)):
-            end_rows(j)
-            own_rows(j)
+        end_rows(2)
+        own_rows(2)
+        end_rows(3)
+        end_rows(4)
+        own_rows(3)
+        own_rows(4)
         for copy in sent + results:
             copy.wait_send()
         for copy in kept:

time: 125 us -> 120 us (0.960)
  Pallas kernels: 117 us -> 112 us
    pallas_call x1, Pallas kernels: 117 us -> 112 us  [product_of(): pl.pallas_call(kernel, out_shape=jax.ShapeDtypeStruct((rows, cols), f32),...]
where the time goes in v3:
time: 120 us
  Pallas kernels  112 us (93%)
  other arithmetic  7.33 us (6%)
    pallas_call x1, Pallas kernels, product_of(): pl.pallas_call(kernel, out_shape=jax.ShapeDtypeStruct((rows, cols), f32),...  112 us
    mul x1, other arithmetic, masked_ham(): ham = hamiltonian[0].reshape(blocks, BLOCK, -1) * wide[:, None, :]  3.26 us
    mul x1, other arithmetic, lined_up(): out = total.reshape(-1, BLOCK, total.shape[1]) * wide[:, None, :]  3.23 us

profile of v3, /device:TPU:0, one launch (start us, length us, event | category | flops | bytes accessed | tf_op | source)
XLA Modules:
  0.0 120.3 jit_solution(15449823309660407172)
XLA Ops:
  0.0 0.7 convert_bitcast_fusion
  0.7 0.1 broadcast_in_dim.14
  0.8 0.1 mul.37
  0.9 0.0 copy-start.2
  0.9 0.0 copy-start
  0.9 3.3 %bitcast_multiply_fusion.1.h_ref = f32[256,2048]{1,0:T(8,128)} fusion(f32[1,256,2048]{2,1,0:T(8,128)} %param.7, f32[4,2048]{1,0:T(4,128)S(1)} %mul.37), kind=kLoop, calls=%fused_computation.1 | loop fusion | flops 524288 | bytes 4227072 | tf_op jit(solution)/shard_map/mul | solution.py:22
  4.2 0.0 copy-done.2
  4.2 0.1 broadcast_in_dim.12
  4.2 0.1 reshape.17
  4.3 0.1 broadcast_in_dim.13
  4.4 0.2 copy.7
  4.6 0.0 copy-done
  4.6 0.1 bitcast_multiply_fusion.2.d_ref
  4.7 0.0 copy-start.1
  4.7 112.1 %shard_map.55 = f32[512,1024]{1,0:T(8,128)} custom-call(f32[512,256]{1,0:T(8,128)S(1)} %bitcast_multiply_fusion.2.d_ref, f32[256,2048]{1,0:T(8,128)} %bitcast_multiply_fusion.1.h_ref), custom_call_target="tpu_custom_call" | custom-call | tf_op jit(solution)/shard_map/pallas_call | solution.py:280
  116.8 0.0 copy-done.1
  116.8 0.1 dynamic-slice_convert_fusion
  116.9 0.1 broadcast_in_dim.15
  117.0 0.1 mul.42
  117.1 3.2 %bitcast_multiply_fusion = f32[512,1024]{1,0:T(8,128)} fusion(f32[512,1024]{1,0:T(8,128)} %shard_map.55, f32[8,1024]{1,0:T(8,128)S(1)} %mul.42), kind=kLoop, calls=%fused_computation | loop fusion | flops 524288 | bytes 4227072 | tf_op jit(solution)/shard_map/mul | solution.py:314
  (1 shorter events, 0.0 us)
Async XLA Ops:
  0.9 3.3 %copy-start.2 = (s32[1,8,4]{1,2,0:T(4,128)S(1)}, s32[1,8,4]{1,2,0:T(4,128)}, u32[]{:S(2)}) copy-start(s32[1,8,4]{1,2,0:T(4,128)} %param.6) | copy-start | bytes 388
  0.9 3.7 %copy-start = (f32[1,512,256]{2,1,0:T(8,128)S(1)}, f32[1,512,256]{2,1,0:T(8,128)}, u32[]{:S(2)}) copy-start(f32[1,512,256]{2,1,0:T(8,128)} %param.5) | copy-start | bytes 1572868
  4.7 112.1 %copy-start.1 = (s32[8,32]{1,0:T(8,128)S(1)}, s32[8,32]{1,0:T(8,128)}, u32[]{:S(2)}) copy-start(s32[8,32]{1,0:T(8,128)} %param.9) | copy-start | bytes 3076

commit v4 on v3

--- a/solution.py
+++ b/solution.py
@@ -29,9 +29,9 @@
 
 
 def kernel(
-    d_ref, h_ref, out_ref,
-    dbuf, hbuf, dhi, dlo, hhi, hlo, mine, ends,
-    d_sem, h_sem, res_sem, send_sem, res_send, local_sem,
+    d_ref, d_mask, h_ref, h_mask, out_ref,
+    dbuf, hbuf, masks, dhi, dlo, hhi, hlo, mine, ends,
+    d_sem, h_sem, res_sem, send_sem, res_send, local_sem, mask_sem,
 ):
     r, c, l = lax.axis_index("row"), lax.axis_index("col"), lax.axis_index("layer")
     rows, width = d_ref.shape
@@ -86,15 +86,21 @@
             pl.semaphore_signal(barrier, inc=1, device_id=where, device_id_type=pl.DeviceIdType.MESH)
         pl.semaphore_wait(barrier, len(partners))
 
+    def mask_dens(half):
+        for i in range(rows // BLOCK):
+            block = pl.ds(half * rows + i * BLOCK, BLOCK)
+            dbuf[own, block, :] = d_ref[pl.ds(i * BLOCK, BLOCK), :] * d_mask[pl.ds(i, 1), :]
+
     y = at(r, c, other)
 
     @pl.when(jnp.logical_not(is_hub))
     def _():
         sent.clear()
         hub = at(1 + r // 3, c, l)
+        mask_dens(1)
         greet([hub, y])
-        push(d_ref, piece(own, 1), d_sem.at[own, 1], hub)
-        push(d_ref, piece(own, 1), d_sem.at[own, 1], y)
+        push(piece(own, 1), piece(own, 1), d_sem.at[own, 1], hub)
+        push(piece(own, 1), piece(own, 1), d_sem.at[own, 1], y)
         for j in range(len(spans)):
             push(ham_from(other, j), held(r, l, j), h_sem.at[r, l, j], y)
         arrived(piece(yours, 1), d_sem.at[yours, 1])
@@ -130,6 +136,7 @@
         far_end = 3 - end_row
         x, s = at(r, across, l), at(r, sibling, l)
         end, far = at(end_row, c, l), at(far_row, c, l)
+        mask_dens(0)
         greet([y, x, s, end, far])
 
         def absorb(slot, half):
@@ -149,6 +156,9 @@
                 push(piece(slot, half), piece(slot, half), d_sem.at[slot, half], where)
             absorb(slot, half)
 
+        def mask_from(layer):
+            return h_mask.at[:, :, pl.ds(pl.multiple_of(layer * cols, cols), cols)]
+
         def straight(j):
             push(ham_from(l, j), held(r, l, j), h_sem.at[r, l, j], far)
 
@@ -166,13 +176,15 @@
                     arrived(held(row, layer, j), h_sem.at[row, layer, j])
 
             def part(i, _):
-                at_rows = pl.ds(pl.multiple_of(i * 256, 256), 256)
-                high, low = split(hbuf[at_rows, chunk(j)])
-                hhi[at_rows, chunk(j)] = high
-                hlo[at_rows, chunk(j)] = low
+                kept_blocks = masks[i // 2, i % 2, :, chunk(j)]
+                for k in range(depth // BLOCK):
+                    at_rows = pl.ds(pl.multiple_of(i * depth + k * BLOCK, BLOCK), BLOCK)
+                    high, low = split(hbuf[at_rows, chunk(j)] * kept_blocks[k : k + 1, :])
+                    hhi[at_rows, chunk(j)] = high
+                    hlo[at_rows, chunk(j)] = low
                 return 0
 
-            lax.fori_loop(0, hbuf.shape[0] // 256, part, 0)
+            lax.fori_loop(0, hbuf.shape[0] // depth, part, 0)
 
         def rows_of(half, target, j):
             def tile(i, _):
@@ -205,10 +217,8 @@
             copy.start()
             kept.append(copy)
 
-        local_d = pltpu.make_async_copy(d_ref, piece(own, 0), local_sem.at[0])
-        local_d.start()
         for where in (y, x, s):
-            push(d_ref, piece(own, 0), d_sem.at[own, 0], where)
+            push(piece(own, 0), piece(own, 0), d_sem.at[own, 0], where)
         straight(0)
         straight(1)
         for j in range(len(spans)):
@@ -218,7 +228,9 @@
             hbuf.at[ham_rows(r, l), :], local_sem.at[1],
         )
         local_h.start()
-        local_d.wait()
+        push(mask_from(other), masks.at[:, l], mask_sem, y)
+        local_mask = pltpu.make_async_copy(mask_from(l), masks.at[:, l], local_sem.at[0])
+        local_mask.start()
         absorb(own, 0)
         take(own, 1, x, s)
         relay(r, other, 0)
@@ -238,6 +250,8 @@
         for slot in beside:
             take(slot, 1)
         local_h.wait()
+        local_mask.wait()
+        arrived(masks.at[:, other], mask_sem)
         end_rows(0)
         relay_end(2)
         take(across * 2 + l, 0, s)
@@ -269,7 +283,7 @@
     return [(sum(widths[:j]), width) for j, width in enumerate(widths)]
 
 
-def product_of(dens, ham, layers, grid_cols):
+def product_of(dens, dens_wide, ham, ham_wide, layers, grid_cols):
     rows, width = dens.shape
     depth, ham_cols = ham.shape
     cols = ham_cols // layers
@@ -280,11 +294,17 @@
     return pl.pallas_call(
         kernel,
         out_shape=jax.ShapeDtypeStruct((rows, cols), f32),
-        in_specs=[pl.BlockSpec(memory_space=pl.ANY)] * 2,
+        in_specs=[
+            pl.BlockSpec(memory_space=pltpu.VMEM),
+            pl.BlockSpec(memory_space=pltpu.VMEM),
+            pl.BlockSpec(memory_space=pl.ANY),
+            pl.BlockSpec(memory_space=pltpu.VMEM),
+        ],
         out_specs=pl.BlockSpec(memory_space=pl.ANY),
         scratch_shapes=[
             pltpu.VMEM((layers * grid_cols, 2 * rows, width), f32),
             pltpu.VMEM((inner, cols), f32),
+            pltpu.VMEM((ham_wide.shape[0], layers, ham_wide.shape[1], cols), f32),
             pltpu.VMEM((2 * rows, inner), bf16),
             pltpu.VMEM((2 * rows, inner), bf16),
             pltpu.VMEM((inner, cols), bf16),
@@ -297,17 +317,19 @@
             dma((16 + 5 * chunks,)),
             dma((chunks,)),
             dma((2 + chunks,)),
+            dma,
         ],
         compiler_params=pltpu.CompilerParams(
             collective_id=0, has_side_effects=True, vmem_limit_bytes=52 * 2**20
         ),
-    )(dens, ham)
+    )(dens, dens_wide, ham, ham_wide)
 
 
 def lined_up(density, dens_mask, hamiltonian, ham_mask, filter_mask, *, layers, grid_cols):
-    dens = density[0] * expand(dens_mask[0])
-    ham = masked_ham(hamiltonian, ham_mask)
-    total = product_of(dens, ham, layers, grid_cols)
+    dens_wide = jnp.repeat(dens_mask[0].astype(jnp.float32), BLOCK, axis=1)
+    ham_wide = jnp.repeat(ham_mask[0].astype(jnp.float32), BLOCK, axis=1)
+    ham_wide = ham_wide.reshape(-1, hamiltonian.shape[1] // BLOCK, hamiltonian.shape[2])
+    total = product_of(density[0], dens_wide, hamiltonian[0], ham_wide, layers, grid_cols)
     kept_blocks = filter_mask.shape[1] // layers
     kept = lax.dynamic_slice_in_dim(filter_mask, lax.axis_index("layer") * kept_blocks, kept_blocks, 1)
     wide = jnp.repeat(kept.astype(jnp.float32), BLOCK, axis=1)

time: 120 us -> 119 us (level)
  other arithmetic: 7.33 us -> 4.69 us
    mul x2 -> x0, other arithmetic: 3.33 us -> none  [the longest x1 3.26 us: masked_ham(): ham = hamiltonian[0].reshape(blocks, BLOCK, -1) * wide[:, None, :]]
where the time goes in v4:
time: 119 us
  Pallas kernels  112 us (94%)
  other arithmetic  4.69 us (4%)
  local copies, waits for them, and re-layouts  1.71 us (1%)
    pallas_call x1, Pallas kernels, product_of(): pl.pallas_call(kernel, out_shape=jax.ShapeDtypeStruct((rows, cols), f32),...  112 us
    mul x1, other arithmetic, lined_up(): out = total.reshape(-1, BLOCK, total.shape[1]) * wide[:, None, :]  3.23 us

profile of v4, /device:TPU:0, one launch (start us, length us, event | category | flops | bytes accessed | tf_op | source)
XLA Modules:
  0.0 118.6 jit_solution(9551741090664330901)
XLA Ops:
  0.0 0.7 convert_bitcast_fusion.1
  0.7 0.1 copy.6
  0.8 0.1 broadcast_in_dim.9
  0.8 0.1 reshape.9.d_mask
  0.9 0.7 convert_bitcast_fusion
  1.6 0.1 broadcast_in_dim.10
  1.8 0.1 reshape_reshape.3.h_mask
  1.9 0.0 copy-start
  1.9 1.0 copy-done
  3.0 0.0 copy-start.1
  3.0 112.2 %shard_map.55 = f32[512,1024]{1,0:T(8,128)} custom-call(f32[512,256]{1,0:T(8,128)S(1)} %bitcast.8, f32[8,256]{1,0:T(8,128)S(1)} %reshape.9.d_mask, f32[256,2048]{1,0:T(8,128)} %bitcast.9, f32[4,4,2048]{2,1,0:T(4,128)S(1)} %reshape_reshape.3.h_mask), custom_call_target="tpu_custom_call" | custom-call | tf_op jit(solution)/shard_map/pallas_call | solution.py:294
  115.2 0.0 copy-done.1
  115.2 0.1 dynamic-slice_convert_fusion
  115.2 0.1 broadcast_in_dim.11
  115.3 0.1 mul.17
  115.4 3.2 %bitcast_multiply_fusion = f32[512,1024]{1,0:T(8,128)} fusion(f32[512,1024]{1,0:T(8,128)} %shard_map.55, f32[8,1024]{1,0:T(8,128)S(1)} %mul.17), kind=kLoop, calls=%fused_computation | loop fusion | flops 524288 | bytes 4227072 | tf_op jit(solution)/shard_map/mul | solution.py:336
Async XLA Ops:
  1.9 1.0 copy-start
  3.0 112.2 %copy-start.1 = (s32[8,32]{1,0:T(8,128)S(1)}, s32[8,32]{1,0:T(8,128)}, u32[]{:S(2)}) copy-start(s32[8,32]{1,0:T(8,128)} %param.9) | copy-start | bytes 3076

commit v5 on v4

--- a/solution.py
+++ b/solution.py
@@ -30,7 +30,7 @@
 
 def kernel(
     d_ref, d_mask, h_ref, h_mask, out_ref,
-    dbuf, hbuf, masks, dhi, dlo, hhi, hlo, mine, ends,
+    dbuf, hbuf, raw, masks, yours_mask, dhi, dlo, hhi, hlo, ends,
     d_sem, h_sem, res_sem, send_sem, res_send, local_sem, mask_sem,
 ):
     r, c, l = lax.axis_index("row"), lax.axis_index("col"), lax.axis_index("layer")
@@ -87,25 +87,29 @@
         pl.semaphore_wait(barrier, len(partners))
 
     def mask_dens(half):
+        load.wait()
         for i in range(rows // BLOCK):
             block = pl.ds(half * rows + i * BLOCK, BLOCK)
-            dbuf[own, block, :] = d_ref[pl.ds(i * BLOCK, BLOCK), :] * d_mask[pl.ds(i, 1), :]
+            dbuf[own, block, :] = raw[pl.ds(i * BLOCK, BLOCK), :] * d_mask[pl.ds(i, 1), :]
 
     y = at(r, c, other)
+    load = pltpu.make_async_copy(d_ref, raw, local_sem.at[0])
+    load.start()
 
     @pl.when(jnp.logical_not(is_hub))
     def _():
         sent.clear()
         hub = at(1 + r // 3, c, l)
+        greet([hub, y])
+        push(ham_from(other, 0), held(r, l, 0), h_sem.at[r, l, 0], y)
         mask_dens(1)
-        greet([hub, y])
         push(piece(own, 1), piece(own, 1), d_sem.at[own, 1], hub)
         push(piece(own, 1), piece(own, 1), d_sem.at[own, 1], y)
-        for j in range(len(spans)):
+        for j in range(1, len(spans)):
             push(ham_from(other, j), held(r, l, j), h_sem.at[r, l, j], y)
         arrived(piece(yours, 1), d_sem.at[yours, 1])
         push(piece(yours, 1), piece(yours, 1), d_sem.at[yours, 1], hub)
-        sent[0].wait_send()
+        sent[1].wait_send()
         last = len(sent) - 1
         for j in range(len(spans)):
             push(ham_from(l, j), held(r, l, j), h_sem.at[r, l, j], hub)
@@ -116,18 +120,13 @@
             else:
                 sent[last + 2 * j - 1].wait_send()
                 sent[last + 2 * j].wait_send()
-        waited = {0} | set(range(last, len(sent) - 2))
-        kept = []
+        waited = {1} | set(range(last, len(sent) - 2))
         for j in range(len(spans)):
             arrived(ends.at[:, chunk(j)], res_sem.at[j])
-            keep = pltpu.make_async_copy(ends.at[:, chunk(j)], out_ref.at[:, chunk(j)], local_sem.at[j])
-            keep.start()
-            kept.append(keep)
+            out_ref[:, chunk(j)] = ends[:, chunk(j)]
         for i, copy in enumerate(sent):
             if i not in waited:
                 copy.wait_send()
-        for copy in kept:
-            copy.wait()
 
     @pl.when(is_hub)
     def _():
@@ -136,7 +135,6 @@
         far_end = 3 - end_row
         x, s = at(r, across, l), at(r, sibling, l)
         end, far = at(end_row, c, l), at(far_row, c, l)
-        mask_dens(0)
         greet([y, x, s, end, far])
 
         def absorb(slot, half):
@@ -156,8 +154,14 @@
                 push(piece(slot, half), piece(slot, half), d_sem.at[slot, half], where)
             absorb(slot, half)
 
-        def mask_from(layer):
-            return h_mask.at[:, :, pl.ds(pl.multiple_of(layer * cols, cols), cols)]
+        def widened(layer):
+            blocks = h_mask.shape[1]
+            at_block = layer * (blocks // 2) + lax.broadcasted_iota(jnp.int32, (blocks, cols), 1) // BLOCK
+            pick = lax.broadcasted_iota(jnp.int32, (blocks, cols), 0) == at_block
+            return jnp.dot(
+                h_mask[...].astype(jnp.float32), pick.astype(jnp.float32),
+                preferred_element_type=jnp.float32,
+            )
 
         def straight(j):
             push(ham_from(l, j), held(r, l, j), h_sem.at[r, l, j], far)
@@ -170,12 +174,9 @@
             relay(end_row, l, j)
             relay(end_row, other, j)
 
-        def split_ham(j):
-            for row in (far_row, far_end):
-                for layer in range(2):
-                    arrived(held(row, layer, j), h_sem.at[row, layer, j])
-
+        def split_ham(first, count, j):
             def part(i, _):
+                i = first + i
                 kept_blocks = masks[i // 2, i % 2, :, chunk(j)]
                 for k in range(depth // BLOCK):
                     at_rows = pl.ds(pl.multiple_of(i * depth + k * BLOCK, BLOCK), BLOCK)
@@ -184,25 +185,40 @@
                     hlo[at_rows, chunk(j)] = low
                 return 0
 
-            lax.fori_loop(0, hbuf.shape[0] // depth, part, 0)
-
-        def rows_of(half, target, j):
+            lax.fori_loop(0, count, part, 0)
+
+        def rows_of(half, target, first, count, j, add):
+            at_depth = pl.ds(pl.multiple_of(first * depth, depth), count * depth)
+
             def tile(i, _):
                 at_rows = pl.ds(pl.multiple_of(half * rows + i * 256, 256), 256)
-                high = dhi[at_rows, :]
-                total = jnp.dot(high, hhi[:, chunk(j)], preferred_element_type=jnp.float32)
-                total += jnp.dot(high, hlo[:, chunk(j)], preferred_element_type=jnp.float32)
-                total += jnp.dot(dlo[at_rows, :], hhi[:, chunk(j)], preferred_element_type=jnp.float32)
-                target[pl.ds(pl.multiple_of(i * 256, 256), 256), chunk(j)] = total
+                to_rows = pl.ds(pl.multiple_of(i * 256, 256), 256)
+                high, h_high = dhi[at_rows, at_depth], hhi[at_depth, chunk(j)]
+                total = jnp.dot(high, h_high, preferred_element_type=jnp.float32)
+                total += jnp.dot(high, hlo[at_depth, chunk(j)], preferred_element_type=jnp.float32)
+                total += jnp.dot(dlo[at_rows, at_depth], h_high, preferred_element_type=jnp.float32)
+                if add:
+                    total += target[to_rows, chunk(j)]
+                target[to_rows, chunk(j)] = total
                 return 0
 
             lax.fori_loop(0, rows // 256, tile, 0)
 
-        results, kept = [], []
-
-        def end_rows(j):
-            split_ham(j)
-            rows_of(1, ends, j)
+        near, near_count = (r - 1) * 2, 6
+        late, late_count = far_end * 2, 2
+        results = []
+
+        def near_end(j):
+            for layer in range(2):
+                arrived(held(far_row, layer, j), h_sem.at[far_row, layer, j])
+            split_ham(near, near_count, j)
+            rows_of(1, ends, near, near_count, j, False)
+
+        def late_end(j):
+            for layer in range(2):
+                arrived(held(far_end, layer, j), h_sem.at[far_end, layer, j])
+            split_ham(late, late_count, j)
+            rows_of(1, ends, late, late_count, j, True)
             copy = pltpu.make_async_remote_copy(
                 src_ref=ends.at[:, chunk(j)], dst_ref=ends.at[:, chunk(j)],
                 send_sem=res_send.at[j], recv_sem=res_sem.at[j],
@@ -211,15 +227,16 @@
             copy.start()
             results.append(copy)
 
-        def own_rows(j):
-            rows_of(0, mine, j)
-            copy = pltpu.make_async_copy(mine.at[:, chunk(j)], out_ref.at[:, chunk(j)], local_sem.at[2 + j])
-            copy.start()
-            kept.append(copy)
-
+        def near_own(j):
+            rows_of(0, out_ref, near, near_count, j, False)
+
+        def late_own(j):
+            rows_of(0, out_ref, late, late_count, j, True)
+
+        straight(0)
+        mask_dens(0)
         for where in (y, x, s):
             push(piece(own, 0), piece(own, 0), d_sem.at[own, 0], where)
-        straight(0)
         straight(1)
         for j in range(len(spans)):
             push(ham_from(other, j), held(r, l, j), h_sem.at[r, l, j], y)
@@ -228,9 +245,12 @@
             hbuf.at[ham_rows(r, l), :], local_sem.at[1],
         )
         local_h.start()
-        push(mask_from(other), masks.at[:, l], mask_sem, y)
-        local_mask = pltpu.make_async_copy(mask_from(l), masks.at[:, l], local_sem.at[0])
-        local_mask.start()
+        wide, wide_other = widened(l), widened(other)
+        for p in range(masks.shape[0]):
+            blocks = slice(p * masks.shape[2], (p + 1) * masks.shape[2])
+            masks[p, l] = wide[blocks]
+            yours_mask[p] = wide_other[blocks]
+        push(yours_mask, masks.at[:, l], mask_sem, y)
         absorb(own, 0)
         take(own, 1, x, s)
         relay(r, other, 0)
@@ -250,31 +270,38 @@
         for slot in beside:
             take(slot, 1)
         local_h.wait()
-        local_mask.wait()
         arrived(masks.at[:, other], mask_sem)
-        end_rows(0)
-        relay_end(2)
+        near_end(0)
+        late_end(0)
         take(across * 2 + l, 0, s)
         take(across * 2 + other, 0, s)
-        end_rows(1)
+        near_end(1)
+        late_end(1)
+        relay_end(2)
+        for slot in beside:
+            take(slot, 0)
+        near_own(0)
+        late_own(0)
+        near_end(2)
         relay_end(3)
         straight(4)
         relay(r, other, 4)
-        for slot in beside:
-            take(slot, 0)
-        own_rows(0)
+        near_own(1)
+        late_own(1)
         relay_end(4)
-        own_rows(1)
-        end_rows(2)
-        own_rows(2)
-        end_rows(3)
-        end_rows(4)
-        own_rows(3)
-        own_rows(4)
+        near_own(2)
+        late_end(2)
+        late_own(2)
+        near_end(3)
+        near_own(3)
+        late_end(3)
+        near_end(4)
+        near_own(4)
+        late_end(4)
+        late_own(3)
+        late_own(4)
         for copy in sent + results:
             copy.wait_send()
-        for copy in kept:
-            copy.wait()
 
 
 def chunk_spans(cols):
@@ -283,11 +310,12 @@
     return [(sum(widths[:j]), width) for j, width in enumerate(widths)]
 
 
-def product_of(dens, dens_wide, ham, ham_wide, layers, grid_cols):
+def product_of(dens, dens_wide, ham, ham_mask, layers, grid_cols):
     rows, width = dens.shape
     depth, ham_cols = ham.shape
     cols = ham_cols // layers
     inner = layers * grid_cols * width
+    planes = inner // (layers * depth)
     chunks = len(chunk_spans(cols))
     f32, bf16 = jnp.float32, jnp.bfloat16
     dma = pltpu.SemaphoreType.DMA
@@ -295,41 +323,40 @@
         kernel,
         out_shape=jax.ShapeDtypeStruct((rows, cols), f32),
         in_specs=[
+            pl.BlockSpec(memory_space=pltpu.HBM),
             pl.BlockSpec(memory_space=pltpu.VMEM),
-            pl.BlockSpec(memory_space=pltpu.VMEM),
-            pl.BlockSpec(memory_space=pl.ANY),
+            pl.BlockSpec(memory_space=pltpu.HBM),
             pl.BlockSpec(memory_space=pltpu.VMEM),
         ],
-        out_specs=pl.BlockSpec(memory_space=pl.ANY),
+        out_specs=pl.BlockSpec(memory_space=pltpu.VMEM),
         scratch_shapes=[
             pltpu.VMEM((layers * grid_cols, 2 * rows, width), f32),
             pltpu.VMEM((inner, cols), f32),
-            pltpu.VMEM((ham_wide.shape[0], layers, ham_wide.shape[1], cols), f32),
+            pltpu.VMEM((rows, width), f32),
+            pltpu.VMEM((planes, layers, depth // BLOCK, cols), f32),
+            pltpu.VMEM((planes, depth // BLOCK, cols), f32),
             pltpu.VMEM((2 * rows, inner), bf16),
             pltpu.VMEM((2 * rows, inner), bf16),
             pltpu.VMEM((inner, cols), bf16),
             pltpu.VMEM((inner, cols), bf16),
-            pltpu.VMEM((rows, cols), f32),
             pltpu.VMEM((rows, cols), f32),
             dma((layers * grid_cols, 2)),
             dma((4, 2, chunks)),
             dma((chunks,)),
             dma((16 + 5 * chunks,)),
             dma((chunks,)),
-            dma((2 + chunks,)),
+            dma((2,)),
             dma,
         ],
         compiler_params=pltpu.CompilerParams(
-            collective_id=0, has_side_effects=True, vmem_limit_bytes=52 * 2**20
+            collective_id=0, has_side_effects=True, vmem_limit_bytes=56 * 2**20
         ),
-    )(dens, dens_wide, ham, ham_wide)
+    )(dens, dens_wide, ham, ham_mask)
 
 
 def lined_up(density, dens_mask, hamiltonian, ham_mask, filter_mask, *, layers, grid_cols):
     dens_wide = jnp.repeat(dens_mask[0].astype(jnp.float32), BLOCK, axis=1)
-    ham_wide = jnp.repeat(ham_mask[0].astype(jnp.float32), BLOCK, axis=1)
-    ham_wide = ham_wide.reshape(-1, hamiltonian.shape[1] // BLOCK, hamiltonian.shape[2])
-    total = product_of(density[0], dens_wide, hamiltonian[0], ham_wide, layers, grid_cols)
+    total = product_of(density[0], dens_wide, hamiltonian[0], ham_mask[0], layers, grid_cols)
     kept_blocks = filter_mask.shape[1] // layers
     kept = lax.dynamic_slice_in_dim(filter_mask, lax.axis_index("layer") * kept_blocks, kept_blocks, 1)
     wide = jnp.repeat(kept.astype(jnp.float32), BLOCK, axis=1)

time: 119 us -> 119 us (level)
    pallas_call x1, Pallas kernels: 112 us -> 113 us  [product_of(): pl.pallas_call(kernel, out_shape=jax.ShapeDtypeStruct((rows, cols), f32),...]
where the time goes in v5:
time: 119 us
  Pallas kernels  113 us (95%)
  other arithmetic  4.67 us (4%)
    pallas_call x1, Pallas kernels, product_of(): pl.pallas_call(kernel, out_shape=jax.ShapeDtypeStruct((rows, cols), f32),...  113 us
    mul x1, other arithmetic, lined_up(): out = total.reshape(-1, BLOCK, total.shape[1]) * wide[:, None, :]  3.23 us

profile of v5, /device:TPU:0, one launch (start us, length us, event | category | flops | bytes accessed | tf_op | source)
XLA Modules:
  0.0 119.1 jit_solution(388877860755515267)
XLA Ops:
  0.0 0.7 convert_bitcast_fusion
  0.7 0.1 copy.6
  0.8 0.8 dynamic-slice_convert_fusion
  1.5 0.1 broadcast_in_dim.6
  1.6 0.7 reshape.8.d_mask
  2.3 0.1 broadcast_in_dim.7
  2.4 0.1 mul.17
  2.4 113.4 %shard_map.55 = f32[512,1024]{1,0:T(8,128)} custom-call(f32[512,256]{1,0:T(8,128)} %bitcast.8, f32[8,256]{1,0:T(8,128)} %reshape.8.d_mask, f32[256,2048]{1,0:T(8,128)} %bitcast.7, s32[16,32]{1,0:T(8,128)} %bitcast.9), custom_call_target="tpu_custom_call" | custom-call | tf_op jit(solution)/shard_map/pallas_call | solution.py:322
  115.8 3.2 %bitcast_multiply_fusion = f32[512,1024]{1,0:T(8,128)} fusion(f32[512,1024]{1,0:T(8,128)} %shard_map.55, f32[8,1024]{1,0:T(8,128)S(1)} %mul.17), kind=kLoop, calls=%fused_computation | loop fusion | flops 524288 | bytes 4227072 | tf_op jit(solution)/shard_map/mul | solution.py:363

commit v6 on v5

--- a/solution.py
+++ b/solution.py
@@ -29,8 +29,8 @@
 
 
 def kernel(
-    d_ref, d_mask, h_ref, h_mask, out_ref,
-    dbuf, hbuf, raw, masks, yours_mask, dhi, dlo, hhi, hlo, ends,
+    d_ref, d_mask, h_ref, h_mask, f_mask, out_ref,
+    dbuf, hbuf, raw, masks, yours_mask, kept, dhi, dlo, hhi, hlo, ends,
     d_sem, h_sem, res_sem, send_sem, res_send, local_sem, mask_sem,
 ):
     r, c, l = lax.axis_index("row"), lax.axis_index("col"), lax.axis_index("layer")
@@ -88,9 +88,27 @@
 
     def mask_dens(half):
         load.wait()
+        block_of = lax.broadcasted_iota(jnp.int32, (1, width), 1) // BLOCK
         for i in range(rows // BLOCK):
+            wide = jnp.zeros((1, width), jnp.float32)
+            for k in range(width // BLOCK):
+                wide = jnp.where(block_of == k, d_mask[k : k + 1, i : i + 1].astype(jnp.float32), wide)
             block = pl.ds(half * rows + i * BLOCK, BLOCK)
-            dbuf[own, block, :] = raw[pl.ds(i * BLOCK, BLOCK), :] * d_mask[pl.ds(i, 1), :]
+            dbuf[own, block, :] = raw[pl.ds(i * BLOCK, BLOCK), :] * wide
+
+    def widened(mask, layer):
+        blocks = mask.shape[1]
+        at_block = layer * (blocks // 2) + lax.broadcasted_iota(jnp.int32, (blocks, cols), 1) // BLOCK
+        pick = lax.broadcasted_iota(jnp.int32, (blocks, cols), 0) == at_block
+        return jnp.dot(
+            mask[...].astype(jnp.float32), pick.astype(jnp.float32),
+            preferred_element_type=jnp.float32,
+        )
+
+    def filtered(source, j):
+        for i in range(rows // BLOCK):
+            block = pl.ds(i * BLOCK, BLOCK)
+            out_ref[block, chunk(j)] = source[block, chunk(j)] * kept[pl.ds(i, 1), chunk(j)]
 
     y = at(r, c, other)
     load = pltpu.make_async_copy(d_ref, raw, local_sem.at[0])
@@ -121,9 +139,10 @@
                 sent[last + 2 * j - 1].wait_send()
                 sent[last + 2 * j].wait_send()
         waited = {1} | set(range(last, len(sent) - 2))
+        kept[...] = widened(f_mask, l)
         for j in range(len(spans)):
             arrived(ends.at[:, chunk(j)], res_sem.at[j])
-            out_ref[:, chunk(j)] = ends[:, chunk(j)]
+            filtered(ends, j)
         for i, copy in enumerate(sent):
             if i not in waited:
                 copy.wait_send()
@@ -153,15 +172,6 @@
             for where in partners:
                 push(piece(slot, half), piece(slot, half), d_sem.at[slot, half], where)
             absorb(slot, half)
-
-        def widened(layer):
-            blocks = h_mask.shape[1]
-            at_block = layer * (blocks // 2) + lax.broadcasted_iota(jnp.int32, (blocks, cols), 1) // BLOCK
-            pick = lax.broadcasted_iota(jnp.int32, (blocks, cols), 0) == at_block
-            return jnp.dot(
-                h_mask[...].astype(jnp.float32), pick.astype(jnp.float32),
-                preferred_element_type=jnp.float32,
-            )
 
         def straight(j):
             push(ham_from(l, j), held(r, l, j), h_sem.at[r, l, j], far)
@@ -232,6 +242,7 @@
 
         def late_own(j):
             rows_of(0, out_ref, late, late_count, j, True)
+            filtered(out_ref, j)
 
         straight(0)
         mask_dens(0)
@@ -245,7 +256,8 @@
             hbuf.at[ham_rows(r, l), :], local_sem.at[1],
         )
         local_h.start()
-        wide, wide_other = widened(l), widened(other)
+        wide, wide_other = widened(h_mask, l), widened(h_mask, other)
+        kept[...] = widened(f_mask, l)
         for p in range(masks.shape[0]):
             blocks = slice(p * masks.shape[2], (p + 1) * masks.shape[2])
             masks[p, l] = wide[blocks]
@@ -275,22 +287,22 @@
         late_end(0)
         take(across * 2 + l, 0, s)
         take(across * 2 + other, 0, s)
+        relay_end(2)
         near_end(1)
-        late_end(1)
-        relay_end(2)
         for slot in beside:
             take(slot, 0)
-        near_own(0)
-        late_own(0)
-        near_end(2)
         relay_end(3)
         straight(4)
         relay(r, other, 4)
+        late_end(1)
+        relay_end(4)
+        near_end(2)
+        near_own(0)
+        late_own(0)
         near_own(1)
         late_own(1)
-        relay_end(4)
+        late_end(2)
         near_own(2)
-        late_end(2)
         late_own(2)
         near_end(3)
         near_own(3)
@@ -310,7 +322,7 @@
     return [(sum(widths[:j]), width) for j, width in enumerate(widths)]
 
 
-def product_of(dens, dens_wide, ham, ham_mask, layers, grid_cols):
+def product_of(dens, dens_mask, ham, ham_mask, filter_mask, layers, grid_cols):
     rows, width = dens.shape
     depth, ham_cols = ham.shape
     cols = ham_cols // layers
@@ -327,6 +339,7 @@
             pl.BlockSpec(memory_space=pltpu.VMEM),
             pl.BlockSpec(memory_space=pltpu.HBM),
             pl.BlockSpec(memory_space=pltpu.VMEM),
+            pl.BlockSpec(memory_space=pltpu.VMEM),
         ],
         out_specs=pl.BlockSpec(memory_space=pltpu.VMEM),
         scratch_shapes=[
@@ -335,6 +348,7 @@
             pltpu.VMEM((rows, width), f32),
             pltpu.VMEM((planes, layers, depth // BLOCK, cols), f32),
             pltpu.VMEM((planes, depth // BLOCK, cols), f32),
+            pltpu.VMEM((rows // BLOCK, cols), f32),
             pltpu.VMEM((2 * rows, inner), bf16),
             pltpu.VMEM((2 * rows, inner), bf16),
             pltpu.VMEM((inner, cols), bf16),
@@ -349,19 +363,15 @@
             dma,
         ],
         compiler_params=pltpu.CompilerParams(
-            collective_id=0, has_side_effects=True, vmem_limit_bytes=56 * 2**20
+            collective_id=0, has_side_effects=True, vmem_limit_bytes=50 * 2**20
         ),
-    )(dens, dens_wide, ham, ham_mask)
+    )(dens, dens_mask, ham, ham_mask, filter_mask)
 
 
 def lined_up(density, dens_mask, hamiltonian, ham_mask, filter_mask, *, layers, grid_cols):
-    dens_wide = jnp.repeat(dens_mask[0].astype(jnp.float32), BLOCK, axis=1)
-    total = product_of(density[0], dens_wide, hamiltonian[0], ham_mask[0], layers, grid_cols)
-    kept_blocks = filter_mask.shape[1] // layers
-    kept = lax.dynamic_slice_in_dim(filter_mask, lax.axis_index("layer") * kept_blocks, kept_blocks, 1)
-    wide = jnp.repeat(kept.astype(jnp.float32), BLOCK, axis=1)
-    out = total.reshape(-1, BLOCK, total.shape[1]) * wide[:, None, :]
-    return out.reshape(total.shape)
+    return product_of(
+        density[0], dens_mask[0].T, hamiltonian[0], ham_mask[0], filter_mask, layers, grid_cols
+    )
 
 
 def gathered(density, dens_mask, hamiltonian, ham_mask, filter_mask):

time: 119 us -> 116 us (0.975)
  other arithmetic: 4.67 us -> 0 us
  local copies, waits for them, and re-layouts: 1 us -> 4.43 us
  Pallas kernels: 113 us -> 111 us
    unnamed x0 -> x9, local copies, waits for them, and re-layouts: none -> 4.43 us
    mul x1 -> x0, other arithmetic: 3.23 us -> none  [lined_up(): out = total.reshape(-1, BLOCK, total.shape[1]) * wide[:, None, :]]
    pallas_call x1, Pallas kernels: 113 us -> 111 us  [product_of(): pl.pallas_call(kernel, out_shape=jax.ShapeDtypeStruct((rows, cols), f32),...]
    convert_element_type x2 -> x0, other arithmetic: 1.44 us -> none  [the longest x1 0.76 us: lined_up(): wide = jnp.repeat(kept.astype(jnp.float32), BLOCK, axis=1)]
where the time goes in v6:
time: 116 us
  Pallas kernels  111 us (96%)
  local copies, waits for them, and re-layouts  4.43 us (4%)
    pallas_call x1, Pallas kernels, product_of(): pl.pallas_call(kernel, out_shape=jax.ShapeDtypeStruct((rows, cols), f32),...  111 us
    unnamed x9, local copies, waits for them, and re-layouts  4.43 us

profile of v6, /device:TPU:0, one launch (start us, length us, event | category | flops | bytes accessed | tf_op | source)
XLA Modules:
  0.0 115.8 jit_solution(17084425906752086591)
XLA Ops:
  0.0 0.0 copy-start
  0.0 1.0 copy-done
  1.0 0.0 copy-start.1
  1.0 0.7 copy-done.1
  1.7 0.0 copy-start.2
  1.7 0.7 copy-done.2
  2.4 0.0 copy-start.3
  2.4 0.7 copy-done.3
  3.1 111.4 %shard_map.55 = f32[512,1024]{1,0:T(8,128)S(1)} custom-call(f32[512,256]{1,0:T(8,128)S(1)} %bitcast.6, s32[4,8]{1,0:T(4,128)S(1)} %bitcast.8, f32[256,2048]{1,0:T(8,128)} %bitcast.9, s32[16,32]{1,0:T(8,128)S(1)} %bitcast.7, s32[8,32]{1,0:T(8,128)S(1)} %copy-done.2), custom_call_target="tpu_custom_call" | custom-call | tf_op jit(solution)/shard_map/pallas_call | solution.py:334
  114.5 1.3 %copy.7 = f32[512,1024]{1,0:T(8,128)} copy(f32[512,1024]{1,0:T(8,128)S(1)} %shard_map.55) | data formatting | bytes 4194304
Async XLA Ops:
  0.0 1.0 copy-start
  1.0 0.7 copy-start.1
  1.7 0.7 copy-start.2
  2.4 0.7 copy-start.3

commit v7 on v6

--- a/solution.py
+++ b/solution.py
@@ -119,26 +119,26 @@
         sent.clear()
         hub = at(1 + r // 3, c, l)
         greet([hub, y])
-        push(ham_from(other, 0), held(r, l, 0), h_sem.at[r, l, 0], y)
         mask_dens(1)
+        push(piece(own, 1), piece(own, 1), d_sem.at[own, 1], y)
         push(piece(own, 1), piece(own, 1), d_sem.at[own, 1], hub)
-        push(piece(own, 1), piece(own, 1), d_sem.at[own, 1], y)
-        for j in range(1, len(spans)):
+        for j in range(len(spans)):
             push(ham_from(other, j), held(r, l, j), h_sem.at[r, l, j], y)
+            if j == 0:
+                sent[0].wait_send()
         arrived(piece(yours, 1), d_sem.at[yours, 1])
         push(piece(yours, 1), piece(yours, 1), d_sem.at[yours, 1], hub)
+        last = len(sent) - 1
         sent[1].wait_send()
-        last = len(sent) - 1
+        sent[last].wait_send()
         for j in range(len(spans)):
             push(ham_from(l, j), held(r, l, j), h_sem.at[r, l, j], hub)
             arrived(held(r, other, j), h_sem.at[r, other, j])
             push(held(r, other, j), held(r, other, j), h_sem.at[r, other, j], hub)
-            if j == 0:
-                sent[last].wait_send()
-            else:
+            if j > 0:
                 sent[last + 2 * j - 1].wait_send()
                 sent[last + 2 * j].wait_send()
-        waited = {1} | set(range(last, len(sent) - 2))
+        waited = {0, 1} | set(range(last, len(sent) - 2))
         kept[...] = widened(f_mask, l)
         for j in range(len(spans)):
             arrived(ends.at[:, chunk(j)], res_sem.at[j])
@@ -244,13 +244,17 @@
             rows_of(0, out_ref, late, late_count, j, True)
             filtered(out_ref, j)
 
+        def swap(j):
+            push(ham_from(other, j), held(r, l, j), h_sem.at[r, l, j], y)
+
         straight(0)
+        swap(0)
+        straight(1)
+        swap(1)
         mask_dens(0)
-        for where in (y, x, s):
+        for where in (x, s):
             push(piece(own, 0), piece(own, 0), d_sem.at[own, 0], where)
-        straight(1)
-        for j in range(len(spans)):
-            push(ham_from(other, j), held(r, l, j), h_sem.at[r, l, j], y)
+        straight(2)
         local_h = pltpu.make_async_copy(
             h_ref.at[:, pl.ds(pl.multiple_of(l * cols, cols), cols)],
             hbuf.at[ham_rows(r, l), :], local_sem.at[1],
@@ -264,13 +268,15 @@
             yours_mask[p] = wide_other[blocks]
         push(yours_mask, masks.at[:, l], mask_sem, y)
         absorb(own, 0)
+        relay(r, other, 0)
+        swap(2)
+        relay(r, other, 1)
+        swap(3)
+        swap(4)
         take(own, 1, x, s)
-        relay(r, other, 0)
-        relay(r, other, 1)
-        straight(2)
+        relay(r, other, 2)
         take(yours, 1, x, s)
-        relay(r, other, 2)
-        take(yours, 0, x, s)
+        push(piece(own, 0), piece(own, 0), d_sem.at[own, 0], y)
         relay_end(0)
         take(across * 2 + l, 1, s)
         straight(3)
@@ -284,10 +290,11 @@
         local_h.wait()
         arrived(masks.at[:, other], mask_sem)
         near_end(0)
+        take(yours, 0, x, s)
         late_end(0)
         take(across * 2 + l, 0, s)
+        relay_end(2)
         take(across * 2 + other, 0, s)
-        relay_end(2)
         near_end(1)
         for slot in beside:
             take(slot, 0)

time: 116 us -> 115 us (level)
  no operation moved by 1% of the time
where the time goes in v7:
time: 115 us
  Pallas kernels  111 us (97%)
  local copies, waits for them, and re-layouts  4.43 us (4%)
    pallas_call x1, Pallas kernels, product_of(): pl.pallas_call(kernel, out_shape=jax.ShapeDtypeStruct((rows, cols), f32),...  111 us
    unnamed x9, local copies, waits for them, and re-layouts  4.43 us

profile of v7, /device:TPU:0, one launch (start us, length us, event | category | flops | bytes accessed | tf_op | source)
XLA Modules:
  0.0 115.2 jit_solution(16184528988077823732)
XLA Ops:
  0.0 0.0 copy-start
  0.0 1.0 copy-done
  1.0 0.0 copy-start.1
  1.0 0.7 copy-done.1
  1.7 0.0 copy-start.2
  1.7 0.7 copy-done.2
  2.4 0.0 copy-start.3
  2.4 0.7 copy-done.3
  3.1 110.7 %shard_map.55 = f32[512,1024]{1,0:T(8,128)S(1)} custom-call(f32[512,256]{1,0:T(8,128)S(1)} %bitcast.6, s32[4,8]{1,0:T(4,128)S(1)} %bitcast.8, f32[256,2048]{1,0:T(8,128)} %bitcast.9, s32[16,32]{1,0:T(8,128)S(1)} %bitcast.7, s32[8,32]{1,0:T(8,128)S(1)} %copy-done.2), custom_call_target="tpu_custom_call" | custom-call | tf_op jit(solution)/shard_map/pallas_call | solution.py:341
  113.8 1.3 %copy.7 = f32[512,1024]{1,0:T(8,128)} copy(f32[512,1024]{1,0:T(8,128)S(1)} %shard_map.55) | data formatting | bytes 4194304
Async XLA Ops:
  0.0 1.0 copy-start
  1.0 0.7 copy-start.1
  1.7 0.7 copy-start.2
  2.4 0.7 copy-start.3

commit v8 on v7

--- a/solution.py
+++ b/solution.py
@@ -29,12 +29,14 @@
 
 
 def kernel(
-    d_ref, d_mask, h_ref, h_mask, f_mask, out_ref,
+    d_ref, h_ref, packed, out_ref,
     dbuf, hbuf, raw, masks, yours_mask, kept, dhi, dlo, hhi, hlo, ends,
     d_sem, h_sem, res_sem, send_sem, res_send, local_sem, mask_sem,
 ):
     r, c, l = lax.axis_index("row"), lax.axis_index("col"), lax.axis_index("layer")
     rows, width = d_ref.shape
+    cut = rows // BLOCK
+    h_mask, f_mask, d_mask = packed.at[2 * cut :], packed.at[:cut], packed.at[cut : 2 * cut]
     depth = h_ref.shape[0]
     cols = out_ref.shape[1]
     spans = chunk_spans(cols)
@@ -329,7 +331,7 @@
     return [(sum(widths[:j]), width) for j, width in enumerate(widths)]
 
 
-def product_of(dens, dens_mask, ham, ham_mask, filter_mask, layers, grid_cols):
+def product_of(dens, ham, packed, layers, grid_cols):
     rows, width = dens.shape
     depth, ham_cols = ham.shape
     cols = ham_cols // layers
@@ -343,9 +345,7 @@
         out_shape=jax.ShapeDtypeStruct((rows, cols), f32),
         in_specs=[
             pl.BlockSpec(memory_space=pltpu.HBM),
-            pl.BlockSpec(memory_space=pltpu.VMEM),
             pl.BlockSpec(memory_space=pltpu.HBM),
-            pl.BlockSpec(memory_space=pltpu.VMEM),
             pl.BlockSpec(memory_space=pltpu.VMEM),
         ],
         out_specs=pl.BlockSpec(memory_space=pltpu.VMEM),
@@ -372,13 +372,15 @@
         compiler_params=pltpu.CompilerParams(
             collective_id=0, has_side_effects=True, vmem_limit_bytes=50 * 2**20
         ),
-    )(dens, dens_mask, ham, ham_mask, filter_mask)
+    )(dens, ham, packed)
 
 
 def lined_up(density, dens_mask, hamiltonian, ham_mask, filter_mask, *, layers, grid_cols):
-    return product_of(
-        density[0], dens_mask[0].T, hamiltonian[0], ham_mask[0], filter_mask, layers, grid_cols
-    )
+    blocks, across = filter_mask.shape
+    small = dens_mask[0].T
+    small = jnp.pad(small, ((0, blocks - small.shape[0]), (0, across - small.shape[1])))
+    packed = jnp.concatenate([filter_mask, small, ham_mask[0]], axis=0)
+    return product_of(density[0], hamiltonian[0], packed, layers, grid_cols)
 
 
 def gathered(density, dens_mask, hamiltonian, ham_mask, filter_mask):

time: 115 us -> 114 us (level)
  local copies, waits for them, and re-layouts: 4.43 us -> 2.36 us
    unnamed x9 -> x3, local copies, waits for them, and re-layouts: 4.43 us -> 2.36 us
where the time goes in v8:
time: 114 us
  Pallas kernels  111 us (97%)
  local copies, waits for them, and re-layouts  2.36 us (2%)
    pallas_call x1, Pallas kernels, product_of(): pl.pallas_call(kernel, out_shape=jax.ShapeDtypeStruct((rows, cols), f32),...  111 us
    unnamed x3, local copies, waits for them, and re-layouts  2.36 us

profile of v8, /device:TPU:0, one launch (start us, length us, event | category | flops | bytes accessed | tf_op | source)
XLA Modules:
  0.0 113.8 jit_solution(5907487658874518782)
XLA Ops:
  0.0 0.7 fusion.packed
  0.7 0.0 copy-start
  0.7 1.0 copy-done
  1.8 110.7 %shard_map.55 = f32[512,1024]{1,0:T(8,128)S(1)} custom-call(f32[512,256]{1,0:T(8,128)S(1)} %bitcast.6, f32[256,2048]{1,0:T(8,128)} %bitcast.7, s32[32,32]{1,0:T(8,128)S(1)} %fusion.packed), custom_call_target="tpu_custom_call" | custom-call | tf_op jit(solution)/shard_map/pallas_call | solution.py:343
  112.5 1.3 %copy.7 = f32[512,1024]{1,0:T(8,128)} copy(f32[512,1024]{1,0:T(8,128)S(1)} %shard_map.55) | data formatting | bytes 4194304
Async XLA Ops:
  0.7 1.0 copy-start

commit v9 on v8

--- a/solution.py
+++ b/solution.py
@@ -317,9 +317,9 @@
         near_own(3)
         late_end(3)
         near_end(4)
-        near_own(4)
         late_end(4)
         late_own(3)
+        near_own(4)
         late_own(4)
         for copy in sent + results:
             copy.wait_send()

time: 114 us -> 114 us (level)
  no operation moved by 1% of the time
where the time goes in v9:
time: 114 us
  Pallas kernels  111 us (97%)
  local copies, waits for them, and re-layouts  2.36 us (2%)
    pallas_call x1, Pallas kernels, product_of(): pl.pallas_call(kernel, out_shape=jax.ShapeDtypeStruct((rows, cols), f32),...  111 us
    unnamed x3, local copies, waits for them, and re-layouts  2.36 us

profile of v9, /device:TPU:0, one launch (start us, length us, event | category | flops | bytes accessed | tf_op | source)
XLA Modules:
  0.0 113.8 jit_solution(7533343617103470441)
XLA Ops:
  0.0 0.7 fusion.packed
  0.7 0.0 copy-start
  0.7 1.0 copy-done
  1.8 110.7 %shard_map.55 = f32[512,1024]{1,0:T(8,128)S(1)} custom-call(f32[512,256]{1,0:T(8,128)S(1)} %bitcast.6, f32[256,2048]{1,0:T(8,128)} %bitcast.7, s32[32,32]{1,0:T(8,128)S(1)} %fusion.packed), custom_call_target="tpu_custom_call" | custom-call | tf_op jit(solution)/shard_map/pallas_call | solution.py:343
  112.5 1.3 %copy.7 = f32[512,1024]{1,0:T(8,128)} copy(f32[512,1024]{1,0:T(8,128)S(1)} %shard_map.55) | data formatting | bytes 4194304
Async XLA Ops:
  0.7 1.0 copy-start
